TPU v7x, 32 devices: a whole 2x2x4 slice. The times are simulated.
32 devices in a mesh: groups: 1, mp: 4 (over x, core), dp: 8 (over z, y).
Axes of the slice: x: 2, y: 2, z: 4, core: 2. Of those that a mesh axis runs over, the one named last changes fastest.
Arguments:
- stream: bfloat16 [1024, 4608], P(('groups', 'mp'), 'dp'), may hold values from -12 to 12
- active_lists: int32 [8, 8], P(('groups', 'mp')), may hold values from -1 to 63, as said below
- enc_weight: bfloat16 [4608, 8192], P('dp', 'mp'), may hold values from -0.09375 to 0.09375
- enc_bias: float32 [8192], P('mp'), may hold values from -3 to 3
- dec_weight: bfloat16 [8192, 4608], P('mp', 'dp'), may hold values from -0.25 to 0.25
- dec_bias: float32 [4608], P('dp'), may hold values from -3 to 3
Outputs:
- grad_enc: bfloat16 [4608, 8192], P(('groups', 'dp'), 'mp')
- grad_enc_bias: float32 [8192], P(('groups', 'mp'))
- grad_dec: bfloat16 [8192, 4608], P(('groups', 'mp'), 'dp')
- errors: bfloat16 [1024, 4608], P(('groups', 'mp'), 'dp')
Inputs may be any that keep to these rules, and one draw needn't show every extreme that they name: `active_lists`: each row names distinct latent blocks; -1 marks an unused entry. Over the rows of one index of mp, at most 8 entries name blocks of one model shard (blocks k * 16 to (k + 1) * 16 - 1), and in every draw some model shard is named exactly 8 times by the rows of every index of mp.
All inputs are finite; a program needn't handle non-finite values.
Results may differ from a plain program's by a relative error of at most 0.0131.
Values may be sent and summed in bfloat16 or wider, within the bound.
A program may use at most 128 MiB of HBM per device.

v0:
```python
import jax
import jax.numpy as jnp
from jax import lax
from jax.sharding import PartitionSpec as P

BLK = 128
TB = 128
LIST = 8
LBLK_DEV = 16


def slot_table(ids_flat, peer_count, capacity, local_blocks):
    is_live = ids_flat >= 0
    owner_id = jnp.where(is_live, ids_flat // local_blocks, -1)
    local_id = jnp.where(is_live, ids_flat % local_blocks, -1)
    onehot = (owner_id[:, None] == jnp.arange(peer_count)[None, :]).astype(jnp.int32)
    before = jnp.sum(onehot * (jnp.cumsum(onehot, axis=0) - 1), axis=1)
    target = jnp.where(is_live, owner_id * capacity + before, -1)
    placed = (target[None, :] == jnp.arange(peer_count * capacity)[:, None]).astype(jnp.int32)
    filled = jnp.sum(placed, axis=1) > 0
    block_of = jnp.sum(placed * (jnp.arange(ids_flat.shape[0]) // LIST)[None, :], axis=1)
    latent = jnp.where(filled, jnp.sum(placed * local_id[None, :], axis=1), -1)
    return (block_of, latent)


def activate(pre_sum, bias_sel, is_live):
    shifted = pre_sum + bias_sel
    keep = is_live[:, None, None] & (shifted > 0)
    return jnp.where(keep, shifted, 0.0).astype(jnp.bfloat16)


def local(stream, active_lists, enc_weight, enc_bias, dec_weight, dec_bias):
    highest = lax.Precision.HIGHEST
    peer_count = lax.axis_size("mp")
    tok_count, feat_width = stream.shape
    block_count = tok_count // TB
    capacity = max(2, 16 * block_count // peer_count)
    slot_count = peer_count * capacity
    stream_blocks = stream.reshape(block_count, TB, feat_width)
    home_block, home_latent = slot_table(active_lists.reshape(-1), peer_count, capacity, LBLK_DEV)
    home_filled = home_latent >= 0
    outgoing = jnp.where(
        home_filled[:, None, None], stream_blocks[home_block], jnp.zeros((), jnp.bfloat16)
    )
    rows_in, latent_in = (
        lax.all_to_all(
            outgoing.reshape(peer_count, capacity, TB, feat_width),
            "mp",
            split_axis=0,
            concat_axis=0,
            tiled=True,
        ),
        lax.all_to_all(
            home_latent.reshape(peer_count, capacity), "mp", split_axis=0, concat_axis=0, tiled=True
        ),
    )
    rows_in = rows_in.reshape(slot_count, TB, feat_width)
    latent_in = latent_in.reshape(slot_count)
    is_live = latent_in >= 0
    block_id = jnp.where(is_live, latent_in, 0)
    enc_sel = jnp.take(enc_weight.reshape(feat_width, LBLK_DEV, BLK), block_id, axis=1)
    dec_sel = jnp.take(dec_weight.reshape(LBLK_DEV, BLK, feat_width), block_id, axis=0)
    bias_sel = jnp.take(enc_bias.reshape(LBLK_DEV, BLK), block_id, axis=0)[:, None, :]
    pre_part = jnp.einsum("rtd,drb->rtb", rows_in, enc_sel, preferred_element_type=jnp.float32)
    pre_sum = lax.psum(pre_part, "dp")
    latents = activate(pre_sum, bias_sel, is_live)
    dec_parts = jnp.einsum(
        "rtb,rbd->rtd", latents, dec_sel, preferred_element_type=jnp.float32
    ).astype(jnp.bfloat16)
    returned = lax.all_to_all(
        dec_parts.reshape(peer_count, capacity, TB, feat_width),
        "mp",
        split_axis=0,
        concat_axis=0,
        tiled=True,
    )
    returned = returned.reshape(slot_count, TB, feat_width)
    collect = (
        (home_block[None, :] == jnp.arange(block_count)[:, None]) & home_filled[None, :]
    ).astype(jnp.bfloat16)
    recon = (
        jnp.einsum("bp,ptd->btd", collect, returned, preferred_element_type=jnp.float32)
        + dec_bias[None, None, :]
    )
    errors = (recon - stream_blocks.astype(jnp.float32)).astype(jnp.bfloat16)
    outgoing_err = jnp.where(
        home_filled[:, None, None], errors[home_block], jnp.zeros((), jnp.bfloat16)
    )
    errors_in = lax.all_to_all(
        outgoing_err.reshape(peer_count, capacity, TB, feat_width),
        "mp",
        split_axis=0,
        concat_axis=0,
        tiled=True,
    )
    errors_in = errors_in.reshape(slot_count, TB, feat_width)
    code_part = jnp.einsum("rtd,rbd->rtb", errors_in, dec_sel, preferred_element_type=jnp.float32)
    code_grad = lax.psum(code_part.astype(jnp.bfloat16), "dp").astype(jnp.float32)
    pre_grad = jnp.where(latents > 0, code_grad / TB, 0.0).astype(jnp.bfloat16)
    onehot_k = ((block_id[:, None] == jnp.arange(LBLK_DEV)[None, :]) & is_live[:, None]).astype(
        jnp.float32
    )
    per_dec = jnp.einsum("rtb,rtd->rbd", latents, errors_in, preferred_element_type=jnp.float32)
    grad_dec = jnp.einsum("rk,rbd->kbd", onehot_k, per_dec, precision=highest) / TB
    grad_dec = grad_dec.reshape(LBLK_DEV * BLK, feat_width).astype(jnp.bfloat16)
    per_enc = jnp.einsum("rtd,rtb->rdb", rows_in, pre_grad, preferred_element_type=jnp.float32)
    grad_enc = jnp.einsum("rk,rdb->dkb", onehot_k, per_enc, precision=highest)
    grad_enc = grad_enc.reshape(feat_width, LBLK_DEV * BLK).astype(jnp.bfloat16)
    grad_bias = jnp.einsum(
        "rk,rb->kb", onehot_k, jnp.sum(pre_grad.astype(jnp.float32), axis=1), precision=highest
    )
    return (
        grad_enc,
        grad_bias.reshape(LBLK_DEV * BLK),
        grad_dec,
        errors.reshape(tok_count, feat_width),
    )


def solution(mesh):
    return jax.shard_map(
        local,
        mesh=mesh,
        in_specs=(
            P(("groups", "mp"), "dp"),
            P(("groups", "mp"), None),
            P("dp", "mp"),
            P("mp"),
            P("mp", "dp"),
            P("dp"),
        ),
        out_specs=(
            P(("groups", "dp"), "mp"),
            P(("groups", "mp")),
            P(("groups", "mp"), "dp"),
            P(("groups", "mp"), "dp"),
        ),
        check_vma=False,
    )
```

profile of v0, /device:TPU:0, one launch (start us, length us, event | category | flops | bytes accessed | tf_op | source)
XLA Modules:
  0.0 441.7 jit_solution(17225794375648530756)
XLA Ops:
  7.2 0.9 reshape.296
  9.2 4.2 all-to-all-start.1
  13.5 1.0 copy_bitcast_fusion.5
  14.5 3.3 gather_fusion
  17.8 4.9 %broadcast_select_fusion.2 = bf16[4,8,128,576]{2,3,1,0:T(8,128)(2,1)} fusion(bf16[4,8,128,576]{2,3,1,0:T(8,128)(2,1)} %bitcast.77, pred[4,8]{1,0:T(4,128)(4,1)S(1)} %ge.71), kind=kLoop, calls=%fused_computation.19 | loop fusion | flops 2359296 | bytes 9437216 | tf_op jit(solution)/shard_map/jit(_where)/select_n | solution.py:42
  22.7 4.9 %all-to-all-start = ((bf16[4,8,128,576]{2,3,1,0:T(8,128)(2,1)}), bf16[4,8,128,576]{2,3,1,0:T(8,128)(2,1)}, u32[]{:S(2)}, u32[]{:S(2)}) async-start(bf16[4,8,128,576]{2,3,1,0:T(8,128)(2,1)} %broadcast_select_fusion.2), calls=%async_computation | async-start | bytes 9437184 | tf_op jit(solution)/shard_map/all_to_all | solution.py:46
  27.7 2.0 copy_bitcast_fusion.3
  31.0 5.1 %gather_fusion.1 = bf16[32,576,128]{2,1,0:T(8,128)(2,1)} fusion(bf16[576,16,128]{2,0,1:T(8,128)(2,1)} %copy_bitcast_fusion.3, s32[1024]{0:T(1024)S(1)} %pad_clamp_fusion), kind=kCustom, calls=%fused_computation.1 | custom fusion | bytes 9437312 | tf_op jit(solution)/shard_map/jit(_take)/gather | solution.py:61
  36.1 45.3 %all-to-all-done = bf16[4,8,128,576]{2,3,1,0:T(8,128)(2,1)} async-done(((bf16[4,8,128,576]{2,3,1,0:T(8,128)(2,1)}), bf16[4,8,128,576]{2,3,1,0:T(8,128)(2,1)}, u32[]{:S(2)}, u32[]{:S(2)}) %all-to-all-start) | async-done | bytes 4718624 | tf_op jit(solution)/shard_map/all_to_all | solution.py:46
  81.5 6.9 %fusion.6 = f32[32,128,128]{2,1,0:T(8,128)} fusion(bf16[32,128,576]{1,2,0:T(8,128)(2,1)} %bitcast.3, bf16[32,576,128]{2,1,0:T(8,128)(2,1)} %gather_fusion.1, pred[32]{0:T(512)(128)(4,1)S(1)} %get-tuple-element.10), kind=kOutput, calls=%fused_computation.11 | convolution fusion | flops 606339072 | bytes 11534368 | tf_op jit(solution)/shard_map/rtd,drb->rtb/dot_general | solution.py:64
  88.3 2.3 copy_bitcast_fusion.2
  91.2 3.3 gather_fusion.3
  94.6 96.5 %all-reduce.3.cloned.1.call-done = f32[32,128,128]{2,1,0:T(8,128)} async-done(((f32[32,128,128]{2,1,0:T(8,128)}), f32[32,128,128]{2,1,0:T(8,128)}) %all-reduce.3.cloned.1.call-update) | async-done | bytes 2097168 | tf_op jit(solution)/shard_map/psum | solution.py:65
  191.1 2.1 select_convert_fusion.1
  193.2 5.9 %convolution_convert_fusion = bf16[32,128,576]{1,2,0:T(8,128)(2,1)} fusion(bf16[32,128,128]{2,1,0:T(8,128)(2,1)S(1)} %select_convert_fusion.1, bf16[32,128,576]{1,2,0:T(8,128)(2,1)} %gather_fusion.3, pred[32]{0:T(512)(128)(4,1)S(1)} %get-tuple-element.10), kind=kOutput, calls=%fused_computation.20 | convolution fusion | flops 608698368 | bytes 10485792 | tf_op jit(solution)/shard_map/rtb,rbd->rtd/dot_general | solution.py:67
  199.1 5.2 %all-to-all-start.2 = ((bf16[4,8,128,576]{2,3,1,0:T(8,128)(2,1)}), bf16[4,8,128,576]{2,3,1,0:T(8,128)(2,1)}, u32[]{:S(2)}, u32[]{:S(2)}) async-start(bf16[4,8,128,576]{2,3,1,0:T(8,128)(2,1)} %bitcast.78), calls=%async_computation.2 | async-start | bytes 9437184 | tf_op jit(solution)/shard_map/all_to_all | solution.py:70
  204.4 53.6 %all-to-all-done.2 = bf16[4,8,128,576]{2,3,1,0:T(8,128)(2,1)} async-done(((bf16[4,8,128,576]{2,3,1,0:T(8,128)(2,1)}), bf16[4,8,128,576]{2,3,1,0:T(8,128)(2,1)}, u32[]{:S(2)}, u32[]{:S(2)}) %all-to-all-start.2) | async-done | bytes 4718624 | tf_op jit(solution)/shard_map/all_to_all | solution.py:70
  258.0 5.2 %fusion.25 = bf16[2,128,576]{1,0,2:T(2,128)(2,1)S(1)} fusion(bf16[4,8,128,576]{2,3,1,0:T(8,128)(2,1)} %all-to-all-done.2, bf16[2,128,576]{1,0,2:T(2,128)(2,1)S(1)} %reshape.297, f32[576]{0:T(1024)S(1)} %copy-done.4, pred[32]{0:T(512)(128)(4,1)S(1)} %get-tuple-element.7, s32[32]{0:T(128)S(1)} %get-tuple-element.5), kind=kOutput, calls=%fused_computation.34 | convolution fusion | flops 10027136 | bytes 5310880 | tf_op jit(solution)/shard_map/bp,ptd->btd/dot_general | solution.py:82
  263.2 3.4 gather_fusion.4
  266.6 4.8 %broadcast_select_fusion.1 = bf16[4,8,128,576]{2,3,1,0:T(8,128)(2,1)} fusion(bf16[4,8,128,576]{2,3,1,0:T(8,128)(2,1)} %bitcast.76, pred[4,8]{1,0:T(4,128)(4,1)S(1)} %ge.71), kind=kLoop, calls=%fused_computation.18 | loop fusion | flops 2359296 | bytes 9437216 | tf_op jit(solution)/shard_map/jit(_where)/select_n | solution.py:86
  271.5 4.9 %all-to-all-start.3 = ((bf16[4,8,128,576]{2,3,1,0:T(8,128)(2,1)}), bf16[4,8,128,576]{2,3,1,0:T(8,128)(2,1)}, u32[]{:S(2)}, u32[]{:S(2)}) async-start(bf16[4,8,128,576]{2,3,1,0:T(8,128)(2,1)} %broadcast_select_fusion.1), calls=%async_computation.3 | async-start | bytes 9437184 | tf_op jit(solution)/shard_map/all_to_all | solution.py:89
  276.5 0.8 copy.71
  277.2 53.0 %all-to-all-done.3 = bf16[4,8,128,576]{2,3,1,0:T(8,128)(2,1)} async-done(((bf16[4,8,128,576]{2,3,1,0:T(8,128)(2,1)}), bf16[4,8,128,576]{2,3,1,0:T(8,128)(2,1)}, u32[]{:S(2)}, u32[]{:S(2)}) %all-to-all-start.3) | async-done | bytes 4718624 | tf_op jit(solution)/shard_map/all_to_all | solution.py:89
  330.3 6.6 %fusion.18 = bf16[32,128,128]{2,1,0:T(8,128)(2,1)} fusion(bf16[32,128,576]{1,2,0:T(8,128)(2,1)} %bitcast.12, bf16[32,128,576]{1,2,0:T(8,128)(2,1)} %gather_fusion.3, pred[32]{0:T(512)(128)(4,1)S(1)} %get-tuple-element.10), kind=kOutput, calls=%fused_computation.31 | convolution fusion | flops 606863360 | bytes 10485792 | tf_op jit(solution)/shard_map/rtd,rbd->rtb/dot_general | solution.py:97
  336.9 3.2 fusion.57
  340.1 11.8 %multiply_convert_fusion = bf16[16,128,576]{1,0,2:T(8,128)(2,1)S(1)} fusion(f32[32,128,576]{1,2,0:T(8,128)S(1)} %fusion.57, s32[32]{0:T(128)S(1)} %broadcast_select_fusion.8, pred[32]{0:T(512)(128)(4,1)S(1)} %get-tuple-element.9), kind=kOutput, calls=%fused_computation.15 | convolution fusion | flops 455345152 | bytes 11796640 | tf_op jit(solution)/shard_map/rk,rbd->kbd/dot_general | solution.py:104
  351.9 2.0 copy.69
  353.9 60.1 %all-reduce.5.cloned.1.call-done = bf16[32,128,128]{2,1,0:T(8,128)(2,1)} async-done(((bf16[32,128,128]{2,1,0:T(8,128)(2,1)}), bf16[32,128,128]{2,1,0:T(8,128)(2,1)}) %all-reduce.5.cloned.1.call-update) | async-done | bytes 1048592 | tf_op jit(solution)/shard_map/psum | solution.py:98
  414.0 2.8 convert_reduce_fusion
  417.5 3.5 fusion.28
  421.0 11.8 %fusion.14 = bf16[576,128,16]{1,2,0:T(8,128)(2,1)S(1)} fusion(f32[32,576,128]{2,1,0:T(8,128)S(1)} %fusion.28, s32[32]{0:T(128)S(1)} %broadcast_select_fusion.8, pred[32]{0:T(512)(128)(4,1)S(1)} %get-tuple-element.9), kind=kOutput, calls=%fused_computation.29 | convolution fusion | flops 454165504 | bytes 11796640 | tf_op jit(solution)/shard_map/rk,rdb->dkb/dot_general | solution.py:107
  432.9 2.0 copy.70
  (39 shorter events, 4.2 us)
Async XLA Ops:
  7.2 20.5 %copy-start = (bf16[576,2048]{1,0:T(8,128)(2,1)S(1)}, bf16[576,2048]{1,0:T(8,128)(2,1)}, u32[]{:S(2)}) copy-start(bf16[576,2048]{1,0:T(8,128)(2,1)} %param.8) | copy-start | bytes 7077892
  9.2 13.5 %all-to-all-start.1 = ((s32[4,1,8]{2,1,0:T(1,128)}), s32[4,1,8]{2,1,0:T(1,128)S(1)}, u32[]{:S(2)}, u32[]{:S(2)}) async-start(s32[4,1,8]{2,1,0:T(1,128)} %bitcast.4), calls=%async_computation.1 | async-start | bytes 4096 | tf_op jit(solution)/shard_map/all_to_all | solution.py:53
  22.7 58.8 %all-to-all-start = ((bf16[4,8,128,576]{2,3,1,0:T(8,128)(2,1)}), bf16[4,8,128,576]{2,3,1,0:T(8,128)(2,1)}, u32[]{:S(2)}, u32[]{:S(2)}) async-start(bf16[4,8,128,576]{2,3,1,0:T(8,128)(2,1)} %broadcast_select_fusion.2), calls=%async_computation | async-start | bytes 9437184 | tf_op jit(solution)/shard_map/all_to_all | solution.py:46
  27.6 163.5 %all-reduce.3.cloned.1.call-start = ((), (), s32[]{:S(2)}) async-start(), calls=%async_computation.4 | async-start | bytes 4194304 | tf_op jit(solution)/shard_map/psum | solution.py:65
  88.3 2.3 copy-start.2
  199.1 5.2 %copy-start.3 = (bf16[256,576]{0,1:T(8,128)(2,1)S(1)}, bf16[256,576]{0,1:T(8,128)(2,1)}, u32[]{:S(2)}) copy-start(bf16[256,576]{0,1:T(8,128)(2,1)} %param.6) | copy-start | bytes 884740
  199.1 58.9 %copy-start.4 = (f32[576]{0:T(1024)S(1)}, f32[576]{0:T(1024)}, u32[]{:S(2)}) copy-start(f32[576]{0:T(1024)} %param.11) | copy-start | bytes 6916
  199.1 58.9 %all-to-all-start.2 = ((bf16[4,8,128,576]{2,3,1,0:T(8,128)(2,1)}), bf16[4,8,128,576]{2,3,1,0:T(8,128)(2,1)}, u32[]{:S(2)}, u32[]{:S(2)}) async-start(bf16[4,8,128,576]{2,3,1,0:T(8,128)(2,1)} %bitcast.78), calls=%async_computation.2 | async-start | bytes 9437184 | tf_op jit(solution)/shard_map/all_to_all | solution.py:70
  271.5 58.8 %all-to-all-start.3 = ((bf16[4,8,128,576]{2,3,1,0:T(8,128)(2,1)}), bf16[4,8,128,576]{2,3,1,0:T(8,128)(2,1)}, u32[]{:S(2)}, u32[]{:S(2)}) async-start(bf16[4,8,128,576]{2,3,1,0:T(8,128)(2,1)} %broadcast_select_fusion.1), calls=%async_computation.3 | async-start | bytes 9437184 | tf_op jit(solution)/shard_map/all_to_all | solution.py:89
  276.4 137.6 %all-reduce.5.cloned.1.call-start = ((), (), s32[]{:S(2)}) async-start(), calls=%async_computation.5 | async-start | bytes 2097152 | tf_op jit(solution)/shard_map/psum | solution.py:98
  421.0 13.9 %copy-start.1 = (bf16[576,2048]{1,0:T(8,128)(2,1)S(1)}, bf16[576,2048]{1,0:T(8,128)(2,1)}, u32[]{:S(2)}) copy-start(bf16[576,2048]{1,0:T(8,128)(2,1)} %param.8) | copy-start | bytes 7077892
Sparse Core Ops, SparseCore 0:
  88.5 102.5 all-reduce.2
  337.0 76.9 all-reduce.4
where the time goes:
time: 442 us
  waiting for transfers between devices  309 us (70%)
  matrix products  55.6 us (13%)
  local copies, waits for them, and re-layouts  28.2 us (6%)
  starting transfers between devices  19.4 us (4%)
  other arithmetic  15.8 us (4%)
  between operations  14.2 us (3%)
    psum x1, waiting for transfers between devices, local(): pre_sum = lax.psum(pre_part, 'dp')  96.5 us
    psum x1, waiting for transfers between devices, local(): lax.psum(code_part.astype(jnp.bfloat16), 'dp').astype(jnp.float32)  60.1 us
    all_to_all x1, waiting for transfers between devices, local(): lax.all_to_all(dec_parts.reshape(peer_count, capacity, TB, feat_width), '...  53.6 us
    all_to_all x1, waiting for transfers between devices, local(): lax.all_to_all(outgoing_err.reshape(peer_count, capacity, TB, feat_width)...  53 us
    all_to_all x1, waiting for transfers between devices, local(): lax.all_to_all(outgoing.reshape(peer_count, capacity, TB, feat_width), 'm...  45.3 us
    dot_general x1, matrix products, local(): grad_enc = jnp.einsum('rk,rdb->dkb', onehot_k, per_enc, precision=highest)  11.8 us
    dot_general x1, matrix products, local(): jnp.einsum('rk,rbd->kbd', onehot_k, per_dec, precision=highest) / TB  11.8 us
  transfers between devices with their start and end apart: 6, of which 5 were waited for; matrix products, arithmetic and copies ran while one was open for 9% of the time, Pallas kernels for 0%

commit v1 on v0

v1 whole, which is shorter than its diff:
```python
import functools

import jax
import jax.numpy as jnp
from jax import lax
from jax.experimental import pallas as pl
from jax.experimental.pallas import tpu as pltpu
from jax.sharding import PartitionSpec as P

BLK = 128
TB = 128
LIST = 8
LBLK_DEV = 16
F32 = jnp.float32
BF16 = jnp.bfloat16
VMEM_BYTES = 48 * 1024 * 1024


class Axis:
    def __init__(self, name, size):
        self.name = name
        self.fars = size // 2
        self.me = lax.axis_index(name)
        self.far = self.me // 2
        self.near = self.me % 2

    def later(self, step):
        return lax.rem(self.far + step, self.fars)

    def index(self, far, near):
        return 2 * far + near

    def sibling(self):
        return self.index(self.far, 1 - self.near)

    def push(self, src, dst, send, recv, target):
        return pltpu.make_async_remote_copy(
            src_ref=src,
            dst_ref=dst,
            send_sem=send,
            recv_sem=recv,
            device_id={self.name: target},
            device_id_type=pl.DeviceIdType.MESH,
        )

    def greet(self, barrier):
        pl.semaphore_signal(
            barrier, inc=1, device_id={self.name: self.sibling()}, device_id_type=pl.DeviceIdType.MESH
        )
        for step in range(1, self.fars):
            pl.semaphore_signal(
                barrier,
                inc=1,
                device_id={self.name: self.index(self.later(step), self.near)},
                device_id_type=pl.DeviceIdType.MESH,
            )
        return self.fars


def gather_start(ax, buf, rows, sems):
    far_send, far_recv, near_send, near_recv = sems
    mine = buf.at[pl.ds(ax.me * rows, rows)]
    copies = []
    for step in range(1, ax.fars):
        peer = ax.later(step)
        copies.append(
            ax.push(mine, mine, far_send.at[peer], far_recv.at[ax.far], ax.index(peer, ax.near))
        )
    copies.append(ax.push(mine, mine, near_send.at[ax.far], near_recv.at[ax.far], ax.sibling()))
    for copy in copies:
        copy.start()
    return copies


def gather_finish(ax, buf, rows, sems, copies):
    far_send, far_recv, near_send, near_recv = sems
    for step in range(1, ax.fars):
        peer = ax.later(ax.fars - step)
        landed = buf.at[pl.ds(ax.index(peer, ax.near) * rows, rows)]
        ax.push(
            landed, landed, far_send.at[peer], far_recv.at[peer], ax.index(peer, ax.near)
        ).wait_recv()
        copy = ax.push(landed, landed, near_send.at[peer], near_recv.at[peer], ax.sibling())
        copy.start()
        copies.append(copy)
    for step in range(ax.fars):
        peer = ax.later(ax.fars - step)
        landed = buf.at[pl.ds(ax.index(peer, 1 - ax.near) * rows, rows)]
        ax.push(
            landed, landed, near_send.at[peer], near_recv.at[peer], ax.sibling()
        ).wait_recv()
    for copy in copies:
        copy.wait_send()


def scatter_sum(ax, produce, away, own, near_in, pair, far_in, sems):
    far_send, far_recv, near_send, near_recv = sems
    copies = []
    for step in range(1, ax.fars + 1):
        peer = ax.later(step)
        produce(ax.index(peer, 1 - ax.near), away, peer)
        copy = ax.push(
            away.at[peer], near_in.at[peer], near_send.at[peer], near_recv.at[peer], ax.sibling()
        )
        copy.start()
        copies.append(copy)
    for step in range(1, ax.fars + 1):
        produce(ax.index(ax.later(step), ax.near), own, ax.later(step))

    def wait_near(peer):
        ax.push(
            near_in.at[peer], near_in.at[peer], near_send.at[peer], near_recv.at[peer], ax.sibling()
        ).wait_recv()

    for step in range(1, ax.fars):
        peer = ax.later(step)
        wait_near(peer)
        pair[peer] = (own[peer] + near_in[peer].astype(F32)).astype(pair.dtype)
        copy = ax.push(
            pair.at[peer],
            far_in.at[ax.far],
            far_send.at[peer],
            far_recv.at[ax.far],
            ax.index(peer, ax.near),
        )
        copy.start()
        copies.append(copy)
    wait_near(ax.far)
    total = own[ax.far] + near_in[ax.far].astype(F32)
    for step in range(1, ax.fars):
        peer = ax.later(ax.fars - step)
        ax.push(
            far_in.at[peer],
            far_in.at[peer],
            far_send.at[peer],
            far_recv.at[peer],
            ax.index(peer, ax.near),
        ).wait_recv()
        total = total + far_in[peer].astype(F32)
    for copy in copies:
        copy.wait_send()
    return total


def gather_kernel(
    n_mp, rows, stream_ref, list_ref, enc_ref, stream_out, list_out, enc_out, buf, lists, *sems
):
    ax = Axis("mp", n_mp)
    barrier = pltpu.get_barrier_semaphore()
    pl.semaphore_wait(barrier, ax.greet(barrier))
    buf[pl.ds(ax.me * rows, rows)] = stream_ref[...]
    lists[pl.ds(ax.me, 1)] = list_ref[...]
    list_copies = gather_start(ax, lists, 1, sems[4:8])
    copies = gather_start(ax, buf, rows, sems[0:4])
    for k in range(LBLK_DEV):
        enc_out[k] = enc_ref[:, k * BLK:(k + 1) * BLK]
    gather_finish(ax, lists, 1, sems[4:8], list_copies)
    gather_finish(ax, buf, rows, sems[0:4], copies)
    stream_out[...] = buf[...]
    list_out[...] = lists[...]


def main_kernel(
    n_mp, n_dp, rows, cap,
    table, hits, stream, enc, dec, enc_bias, dec_bias,
    lat_out, pg_out, err_all_out, err_out,
    lat, pg, err, picked, picked_dec,
    pre_away, pre_own, pre_near, pre_pair, pre_far,
    dec_away, dec_own, dec_near, dec_pair, dec_far,
    code_away, code_own, code_near, code_pair, code_far,
    *sems,
):
    mp = Axis("mp", n_mp)
    dp = Axis("dp", n_dp)
    per = n_mp * cap // n_dp
    barrier = pltpu.get_barrier_semaphore()
    count = mp.greet(barrier) + dp.greet(barrier)
    pl.semaphore_wait(barrier, count)

    def group(i):
        return sems[4 * i:4 * i + 4]

    def produce_pre(chunk, dest, place):
        def one(i, _):
            slot = chunk * per + i
            dest[place, i] = jnp.dot(
                stream[table[0, slot]], enc[table[1, slot]], preferred_element_type=F32
            )
            return 0

        lax.fori_loop(0, per, one, 0)

    pre_sum = scatter_sum(
        dp, produce_pre, pre_away, pre_own, pre_near, pre_pair, pre_far, group(0)
    )
    for i in range(per):
        slot = dp.me * per + i
        shifted = pre_sum[i] + enc_bias[table[1, slot]]
        live = jnp.sum(hits[slot], axis=0, keepdims=True)
        lat[slot] = (jnp.maximum(shifted, 0.0) * live).astype(BF16)
    gather_finish(dp, lat, per, group(1), gather_start(dp, lat, per, group(1)))

    def produce_dec(home, dest, place):
        for c in range(cap):
            slot = home * cap + c
            picked_dec[c * BLK:(c + 1) * BLK, :] = dec[table[1, slot]]
            block = lat[slot]
            for j in range(rows):
                hit = jnp.broadcast_to(hits[slot, j:j + 1], (TB, BLK)).astype(BF16)
                picked[j * TB:(j + 1) * TB, c * BLK:(c + 1) * BLK] = block * hit
        out = jnp.dot(picked[...], picked_dec[...], preferred_element_type=F32)
        dest[place] = out.reshape(dest.shape[1:]).astype(dest.dtype)

    recon = scatter_sum(
        mp, produce_dec, dec_away, dec_own, dec_near, dec_pair, dec_far, group(2)
    )
    recon = recon + dec_bias[...][None]
    mine = (recon - stream[pl.ds(mp.me * rows, rows)].astype(F32)).astype(BF16)
    err[pl.ds(mp.me * rows, rows)] = mine
    copies = gather_start(mp, err, rows, group(3))
    err_out[...] = mine
    lat_out[...] = lat[...]
    gather_finish(mp, err, rows, group(3), copies)

    def produce_code(chunk, dest, place):
        def one(i, _):
            slot = chunk * per + i
            dest[place, i] = lax.dot_general(
                err[table[0, slot]],
                dec[table[1, slot]],
                (((1,), (1,)), ((), ())),
                preferred_element_type=F32,
            ).astype(dest.dtype)
            return 0

        lax.fori_loop(0, per, one, 0)

    code = scatter_sum(
        dp, produce_code, code_away, code_own, code_near, code_pair, code_far, group(4)
    )
    for i in range(per):
        slot = dp.me * per + i
        on = lat[slot].astype(F32) > 0
        pg[slot] = jnp.where(on, code[i] * (1.0 / TB), 0.0).astype(BF16)
    copies = gather_start(dp, pg, per, group(5))
    err_all_out[...] = err[...]
    gather_finish(dp, pg, per, group(5), copies)
    pg_out[...] = pg[...]


def grad_kernel(
    slots, table, stream, err, lat, pg, genc, gbias, gdec, acc_enc, acc_dec
):
    acc_enc[...] = jnp.zeros_like(acc_enc)
    acc_dec[...] = jnp.zeros_like(acc_dec)
    gbias[...] = jnp.zeros_like(gbias)
    contract = (((0,), (0,)), ((), ()))

    def one(slot, _):
        block, where = table[0, slot], table[1, slot]
        pg_block = pg[slot]
        acc_dec[where] += lax.dot_general(
            lat[slot], err[block], contract, preferred_element_type=F32
        )
        acc_enc[where] += lax.dot_general(
            stream[block], pg_block, contract, preferred_element_type=F32
        )
        gbias[pl.ds(where, 1), :] += jnp.sum(pg_block.astype(F32), axis=0, keepdims=True)
        return 0

    lax.fori_loop(0, slots, one, 0)
    for k in range(LBLK_DEV):
        genc[:, k * BLK:(k + 1) * BLK] = acc_enc[k].astype(BF16)
        gdec[k] = (acc_dec[k] * (1.0 / TB)).astype(BF16)


def local(n_mp, n_dp, stream, active_lists, enc_weight, enc_bias, dec_weight, dec_bias):
    tok_count, feat = stream.shape
    rows = tok_count // TB
    cap = max(2, 16 * rows // n_mp)
    slots = n_mp * cap
    per = slots // n_dp
    blocks = n_mp * rows
    mps, dps = n_mp // 2, n_dp // 2
    vmem = pl.BlockSpec(memory_space=pltpu.VMEM)
    smem = pl.BlockSpec(memory_space=pltpu.SMEM)
    dma = pltpu.SemaphoreType.DMA
    shape = jax.ShapeDtypeStruct

    lists = jnp.full((1, 8, 128), -1, jnp.int32).at[0, :rows, :LIST].set(active_lists)
    stream_all, lists_all, enc_blocks = pl.pallas_call(
        functools.partial(gather_kernel, n_mp, rows),
        out_shape=(
            shape((blocks, TB, feat), BF16),
            shape((n_mp, 8, 128), jnp.int32),
            shape((LBLK_DEV, feat, BLK), BF16),
        ),
        in_specs=[vmem] * 3,
        out_specs=(vmem,) * 3,
        scratch_shapes=[
            pltpu.VMEM((blocks, TB, feat), BF16),
            pltpu.VMEM((n_mp, 8, 128), jnp.int32),
        ] + [dma((mps,))] * 8,
        compiler_params=pltpu.CompilerParams(
            collective_id=0, has_side_effects=True, vmem_limit_bytes=VMEM_BYTES
        ),
    )(stream.reshape(rows, TB, feat), lists, enc_weight)

    ids = lists_all[:, :rows, :LIST].reshape(n_mp, rows * LIST)
    entry = jnp.arange(rows * LIST)
    mine = (ids >= 0) & (ids // LBLK_DEV == lax.axis_index("mp"))
    before = jnp.sum(mine[:, None, :] & (entry[None, :] < entry[:, None])[None], axis=2)
    placed = mine[:, None, :] & (before[:, None, :] == jnp.arange(cap)[None, :, None])
    home = jnp.arange(n_mp)[:, None, None] * rows
    table = jnp.stack([
        jnp.sum(jnp.where(placed, entry // LIST, 0), axis=2) + home[:, :, 0],
        jnp.sum(jnp.where(placed, (ids % LBLK_DEV)[:, None, :], 0), axis=2),
    ]).reshape(2, slots).astype(jnp.int32)
    in_row = (entry // LIST)[None, :] == jnp.arange(rows)[:, None]
    hits = jnp.sum((placed[:, :, None, :] & in_row).astype(F32), axis=3)
    hits = jnp.broadcast_to(hits.reshape(slots, rows, 1), (slots, rows, BLK))

    small = (TB, BLK)
    wide = (rows, TB, feat)
    lat, pg, err_all, errors = pl.pallas_call(
        functools.partial(main_kernel, n_mp, n_dp, rows, cap),
        out_shape=(
            shape((slots,) + small, BF16),
            shape((slots,) + small, BF16),
            shape((blocks, TB, feat), BF16),
            shape(wide, BF16),
        ),
        in_specs=[smem] + [vmem] * 6,
        out_specs=(vmem,) * 4,
        scratch_shapes=[
            pltpu.VMEM((slots,) + small, BF16),
            pltpu.VMEM((slots,) + small, BF16),
            pltpu.VMEM((blocks, TB, feat), BF16),
            pltpu.VMEM((tok_count, cap * BLK), BF16),
            pltpu.VMEM((cap * BLK, feat), BF16),
        ]
        + [pltpu.VMEM((dps, per) + small, F32)] * 5
        + [pltpu.VMEM((mps,) + wide, t) for t in (BF16, F32, BF16, BF16, BF16)]
        + [pltpu.VMEM((dps, per) + small, t) for t in (BF16, F32, BF16, BF16, BF16)]
        + [dma((dps,))] * 8 + [dma((mps,))] * 8 + [dma((dps,))] * 8,
        compiler_params=pltpu.CompilerParams(
            collective_id=1, has_side_effects=True, vmem_limit_bytes=VMEM_BYTES
        ),
    )(
        table,
        hits,
        stream_all,
        enc_blocks,
        dec_weight.reshape(LBLK_DEV, BLK, feat),
        enc_bias.reshape(LBLK_DEV, 1, BLK),
        dec_bias.reshape(1, feat),
    )

    grad_enc, grad_bias, grad_dec = pl.pallas_call(
        functools.partial(grad_kernel, slots),
        out_shape=(
            shape((feat, LBLK_DEV * BLK), BF16),
            shape((LBLK_DEV, BLK), F32),
            shape((LBLK_DEV, BLK, feat), BF16),
        ),
        in_specs=[smem] + [vmem] * 4,
        out_specs=(vmem,) * 3,
        scratch_shapes=[
            pltpu.VMEM((LBLK_DEV, feat, BLK), F32),
            pltpu.VMEM((LBLK_DEV, BLK, feat), F32),
        ],
        compiler_params=pltpu.CompilerParams(vmem_limit_bytes=VMEM_BYTES),
    )(table, stream_all, err_all, lat, pg)
    return (
        grad_enc,
        grad_bias.reshape(LBLK_DEV * BLK),
        grad_dec.reshape(LBLK_DEV * BLK, feat),
        errors.reshape(tok_count, feat),
    )


def solution(mesh):
    return jax.shard_map(
        functools.partial(local, mesh.shape["mp"], mesh.shape["dp"]),
        mesh=mesh,
        in_specs=(
            P(("groups", "mp"), "dp"),
            P(("groups", "mp"), None),
            P("dp", "mp"),
            P("mp"),
            P("mp", "dp"),
            P("dp"),
        ),
        out_specs=(
            P(("groups", "dp"), "mp"),
            P(("groups", "mp")),
            P(("groups", "mp"), "dp"),
            P(("groups", "mp"), "dp"),
        ),
        check_vma=False,
    )
```

time: 442 us -> 164 us (0.37)
  waiting for transfers between devices: 309 us -> 0 us
  Pallas kernels: 0 us -> 146 us
  matrix products: 55.6 us -> 0 us
  starting transfers between devices: 19.4 us -> 0 us
  other arithmetic: 15.8 us -> 0.54 us
  local copies, waits for them, and re-layouts: 28.2 us -> 14.1 us
  between operations: 14.2 us -> 0.73 us
    psum x2 -> x0, waiting for transfers between devices: 157 us -> none  [the longest x1 96.5 us: local(): pre_sum = lax.psum(pre_part, 'dp')]
    all_to_all x4 -> x0, waiting for transfers between devices: 152 us -> none  [the longest x1 53.6 us: local(): lax.all_to_all(dec_parts.reshape(peer_count, capacity, TB, feat_width), '...]
    pallas_call x0 -> x3, Pallas kernels: none -> 146 us  [the longest x1 118 us: local(): pl.pallas_call(functools.partial(main_kernel, n_mp, n_dp, rows, cap), out...]
    dot_general x9 -> x0, matrix products: 55.6 us -> none  [the longest x1 11.8 us: local(): grad_enc = jnp.einsum('rk,rdb->dkb', onehot_k, per_enc, precision=highest)]
    all_to_all x4 -> x0, starting transfers between devices: 19.3 us -> none  [the longest x1 5.23 us: local(): lax.all_to_all(dec_parts.reshape(peer_count, capacity, TB, feat_width), '...]
    gather x5 -> x0, local copies, waits for them, and re-layouts: 15.6 us -> none  [the longest x1 5.05 us: local(): jnp.take(enc_weight.reshape(feat_width, LBLK_DEV, BLK), block_id, axis=1)]
    select_n x8 -> x2, other arithmetic: 9.83 us -> 0.01 us  [the longest x1 0.01 us: local(): ids % LBLK_DEV]
    unnamed x13 -> x8, local copies, waits for them, and re-layouts: 4.81 us -> 12.1 us
  transfers between devices with their start and end apart: 6 -> 0, of which waited for: 5 -> 0; matrix products, arithmetic and copies ran while one was open for 9% -> 0% of each run, Pallas kernels for 0% -> 0%
where the time goes in v1:
time: 164 us; the launch traced here: 161 us
  Pallas kernels  146 us (89%)
  local copies, waits for them, and re-layouts  14.1 us (9%)
    pallas_call x1, Pallas kernels, local(): pl.pallas_call(functools.partial(main_kernel, n_mp, n_dp, rows, cap), out...  118 us
    pallas_call x1, Pallas kernels, local(): pl.pallas_call(functools.partial(gather_kernel, n_mp, rows), out_shape=(s...  14.6 us
    pallas_call x1, Pallas kernels, local(): pl.pallas_call(functools.partial(grad_kernel, slots), out_shape=(shape((f...  13 us
    unnamed x8, local copies, waits for them, and re-layouts  12.1 us

profile of v1, /device:TPU:0, one launch (start us, length us, event | category | flops | bytes accessed | tf_op | source)
XLA Modules:
  0.0 161.2 jit_solution(14758048901035035371)
XLA Ops:
  0.7 0.1 add.42
  0.7 0.1 add.43
  0.8 0.7 reshape.218.dec_bias
  1.5 0.7 scatter.4.list_ref
  2.2 1.2 copy.15
  3.4 4.3 %copy.18 = bf16[2048,576]{1,0:T(8,128)(2,1)} copy(bf16[2048,576]{0,1:T(8,128)(2,1)} %param.12) | data formatting | bytes 4718592 | tf_op args[4]
  7.7 0.0 copy-start.1
  7.7 14.6 %shard_map.93 = (bf16[8,128,576]{2,1,0:T(8,128)(2,1)S(1)}, s32[4,8,128]{2,1,0:T(8,128)S(1)}, bf16[16,576,128]{2,1,0:T(8,128)(2,1)S(1)}) custom-call(bf16[2,128,576]{2,1,0:T(8,128)(2,1)S(1)} %bitcast.10, s32[1,8,128]{2,1,0:T(8,128)S(1)} %scatter.4.list_ref, bf16[576,2048]{1,0:T(8,128)(2,1)} %enc_ref.1), custom_call_target="tpu_custom_call" | custom-call | tf_op jit(solution)/shard_map/pallas_call | solution.py:291
  22.3 0.0 copy-start
  22.3 1.4 copy-done
  23.7 0.1 reshape.215
  23.8 0.1 convert_reduce_fusion.1
  24.0 0.2 select_reduce_fusion.1
  24.2 0.1 reduce_sum.40
  24.3 0.1 stack.7
  24.4 0.1 convert_reduce_fusion
  24.5 0.1 copy.21
  24.6 0.1 broadcast_in_dim.26.hits
  24.7 0.0 copy-done.1
  24.7 118.2 %shard_map.94 = (bf16[32,128,128]{2,1,0:T(8,128)(2,1)S(1)}, bf16[32,128,128]{2,1,0:T(8,128)(2,1)S(1)}, bf16[8,128,576]{2,1,0:T(8,128)(2,1)S(1)}, bf16[2,128,576]{2,1,0:T(8,128)(2,1)S(1)}) custom-call(s32[2,32]{1,0:T(2,128)S(1)} %pad_add_fusion.table, f32[32,2,128]{2,1,0:T(2,128)S(1)} %broadcast_in_dim.26.hits, ...), custom_call_target="tpu_custom_call" | custom-call | tf_op jit(solution)/shard_map/pallas_call | solution.py:325
  143.0 13.0 %shard_map.95 = (bf16[576,2048]{1,0:T(8,128)(2,1)}, f32[16,128]{1,0:T(8,128)}, bf16[16,128,576]{2,1,0:T(8,128)(2,1)}) custom-call(s32[2,32]{1,0:T(2,128)S(1)} %pad_add_fusion.table, bf16[8,128,576]{2,1,0:T(8,128)(2,1)S(1)} %get-tuple-element.27.stream, bf16[8,128,576]{2,1,0:T(8,128)(2,1)S(1)} %get-tuple-element.29.err, ...), custom_call_target="tpu_custom_call" | custom-call | tf_op jit(solution)/shard_map/pallas_call | solution.py:359
  156.0 0.9 copy.20
  156.9 4.3 %copy.19 = bf16[2048,576]{0,1:T(8,128)(2,1)} copy(bf16[2048,576]{1,0:T(8,128)(2,1)} %bitcast.14) | data formatting | bytes 4718592
  (10 shorter events, 0.1 us)
Async XLA Ops:
  7.7 17.0 %copy-start.1 = (f32[2048]{0:T(1024)S(1)}, f32[2048]{0:T(1024)}, u32[]{:S(2)}) copy-start(f32[2048]{0:T(1024)} %param.11) | copy-start | bytes 24580
  22.3 1.4 copy-start

commit v2 on v1

--- a/solution.py
+++ b/solution.py
@@ -72,8 +72,9 @@
     return copies
 
 
-def gather_finish(ax, buf, rows, sems, copies):
+def gather_finish(ax, buf, rows, sems, copies, work=lambda step: None):
     far_send, far_recv, near_send, near_recv = sems
+    work(0)
     for step in range(1, ax.fars):
         peer = ax.later(ax.fars - step)
         landed = buf.at[pl.ds(ax.index(peer, ax.near) * rows, rows)]
@@ -83,6 +84,7 @@
         copy = ax.push(landed, landed, near_send.at[peer], near_recv.at[peer], ax.sibling())
         copy.start()
         copies.append(copy)
+        work(step)
     for step in range(ax.fars):
         peer = ax.later(ax.fars - step)
         landed = buf.at[pl.ds(ax.index(peer, 1 - ax.near) * rows, rows)]
@@ -143,28 +145,38 @@
 
 
 def gather_kernel(
-    n_mp, rows, stream_ref, list_ref, enc_ref, stream_out, list_out, enc_out, buf, lists, *sems
+    n_mp, rows, stream_ref, list_ref, enc_ref, dec_ref,
+    stream_out, list_out, enc_out, dec_out, buf, lists, *sems
 ):
     ax = Axis("mp", n_mp)
     barrier = pltpu.get_barrier_semaphore()
-    pl.semaphore_wait(barrier, ax.greet(barrier))
-    buf[pl.ds(ax.me * rows, rows)] = stream_ref[...]
+    greeted = ax.greet(barrier)
+    for j in range(rows):
+        buf[ax.me * rows + j] = stream_ref[:, j * TB:(j + 1) * TB].T
+    pl.semaphore_wait(barrier, greeted)
     lists[pl.ds(ax.me, 1)] = list_ref[...]
     list_copies = gather_start(ax, lists, 1, sems[4:8])
     copies = gather_start(ax, buf, rows, sems[0:4])
     for k in range(LBLK_DEV):
         enc_out[k] = enc_ref[:, k * BLK:(k + 1) * BLK]
+        dec_out[k] = dec_ref[:, k * BLK:(k + 1) * BLK].T
     gather_finish(ax, lists, 1, sems[4:8], list_copies)
     gather_finish(ax, buf, rows, sems[0:4], copies)
     stream_out[...] = buf[...]
     list_out[...] = lists[...]
 
 
+def spread_pair(blocks, pair, where, held, spread):
+    for b in range(blocks):
+        for i in range(2):
+            spread[b * TB:(b + 1) * TB, i * BLK:(i + 1) * BLK] = held[where[b, 2 * pair + i]]
+
+
 def main_kernel(
     n_mp, n_dp, rows, cap,
-    table, hits, stream, enc, dec, enc_bias, dec_bias,
-    lat_out, pg_out, err_all_out, err_out,
-    lat, pg, err, picked, picked_dec,
+    table, where, hits, stream, enc, dec, enc_bias, dec_bias,
+    pg_out, stream_out, gdec_out, err_out,
+    lat, pg, err, picked, picked_dec, err_wide, spread,
     pre_away, pre_own, pre_near, pre_pair, pre_far,
     dec_away, dec_own, dec_near, dec_pair, dec_far,
     code_away, code_own, code_near, code_pair, code_far,
@@ -175,6 +187,9 @@
     per = n_mp * cap // n_dp
     barrier = pltpu.get_barrier_semaphore()
     count = mp.greet(barrier) + dp.greet(barrier)
+    empty = jnp.zeros((TB, BLK), BF16)
+    lat[n_mp * cap] = empty
+    pg[n_mp * cap] = empty
     pl.semaphore_wait(barrier, count)
 
     def group(i):
@@ -218,8 +233,10 @@
     mine = (recon - stream[pl.ds(mp.me * rows, rows)].astype(F32)).astype(BF16)
     err[pl.ds(mp.me * rows, rows)] = mine
     copies = gather_start(mp, err, rows, group(3))
-    err_out[...] = mine
-    lat_out[...] = lat[...]
+    for j in range(rows):
+        err_out[:, j * TB:(j + 1) * TB] = mine[j].T
+    for b in range(n_mp * rows):
+        stream_out[:, b * TB:(b + 1) * TB] = stream[b].T
     gather_finish(mp, err, rows, group(3), copies)
 
     def produce_code(chunk, dest, place):
@@ -243,35 +260,29 @@
         on = lat[slot].astype(F32) > 0
         pg[slot] = jnp.where(on, code[i] * (1.0 / TB), 0.0).astype(BF16)
     copies = gather_start(dp, pg, per, group(5))
-    err_all_out[...] = err[...]
-    gather_finish(dp, pg, per, group(5), copies)
+    blocks = n_mp * rows
+    for b in range(blocks):
+        err_wide[:, b * TB:(b + 1) * TB] = err[b].T
+    share = LBLK_DEV // 2 // dp.fars
+
+    def grad_dec(step):
+        def one(pair, _):
+            spread_pair(blocks, pair, where, lat, spread)
+            total = jnp.dot(err_wide[...], spread[...], preferred_element_type=F32)
+            lane = pl.multiple_of(pair * 2 * BLK, 2 * BLK)
+            gdec_out[:, pl.ds(lane, 2 * BLK)] = (total * (1.0 / TB)).astype(BF16)
+            return 0
+
+        lax.fori_loop(step * share, (step + 1) * share, one, 0)
+
+    gather_finish(dp, pg, per, group(5), copies, grad_dec)
     pg_out[...] = pg[...]
 
 
-def grad_kernel(
-    slots, table, stream, err, lat, pg, genc, gbias, gdec, acc_enc, acc_dec
-):
-    acc_enc[...] = jnp.zeros_like(acc_enc)
-    acc_dec[...] = jnp.zeros_like(acc_dec)
-    gbias[...] = jnp.zeros_like(gbias)
-    contract = (((0,), (0,)), ((), ()))
-
-    def one(slot, _):
-        block, where = table[0, slot], table[1, slot]
-        pg_block = pg[slot]
-        acc_dec[where] += lax.dot_general(
-            lat[slot], err[block], contract, preferred_element_type=F32
-        )
-        acc_enc[where] += lax.dot_general(
-            stream[block], pg_block, contract, preferred_element_type=F32
-        )
-        gbias[pl.ds(where, 1), :] += jnp.sum(pg_block.astype(F32), axis=0, keepdims=True)
-        return 0
-
-    lax.fori_loop(0, slots, one, 0)
-    for k in range(LBLK_DEV):
-        genc[:, k * BLK:(k + 1) * BLK] = acc_enc[k].astype(BF16)
-        gdec[k] = (acc_dec[k] * (1.0 / TB)).astype(BF16)
+def grad_kernel(blocks, where, stream, pg, genc, gbias, spread):
+    spread_pair(blocks, pl.program_id(0), where, pg, spread)
+    genc[...] = jnp.dot(stream[...], spread[...], preferred_element_type=F32).astype(BF16)
+    gbias[...] = jnp.sum(spread[...].astype(F32), axis=0, keepdims=True)
 
 
 def local(n_mp, n_dp, stream, active_lists, enc_weight, enc_bias, dec_weight, dec_bias):
@@ -288,15 +299,16 @@
     shape = jax.ShapeDtypeStruct
 
     lists = jnp.full((1, 8, 128), -1, jnp.int32).at[0, :rows, :LIST].set(active_lists)
-    stream_all, lists_all, enc_blocks = pl.pallas_call(
+    stream_all, lists_all, enc_blocks, dec_blocks = pl.pallas_call(
         functools.partial(gather_kernel, n_mp, rows),
         out_shape=(
             shape((blocks, TB, feat), BF16),
             shape((n_mp, 8, 128), jnp.int32),
             shape((LBLK_DEV, feat, BLK), BF16),
-        ),
-        in_specs=[vmem] * 3,
-        out_specs=(vmem,) * 3,
+            shape((LBLK_DEV, BLK, feat), BF16),
+        ),
+        in_specs=[vmem] * 4,
+        out_specs=(vmem,) * 4,
         scratch_shapes=[
             pltpu.VMEM((blocks, TB, feat), BF16),
             pltpu.VMEM((n_mp, 8, 128), jnp.int32),
@@ -304,7 +316,7 @@
         compiler_params=pltpu.CompilerParams(
             collective_id=0, has_side_effects=True, vmem_limit_bytes=VMEM_BYTES
         ),
-    )(stream.reshape(rows, TB, feat), lists, enc_weight)
+    )(stream.T, lists, enc_weight, dec_weight.T)
 
     ids = lists_all[:, :rows, :LIST].reshape(n_mp, rows * LIST)
     entry = jnp.arange(rows * LIST)
@@ -320,24 +332,34 @@
     hits = jnp.sum((placed[:, :, None, :] & in_row).astype(F32), axis=3)
     hits = jnp.broadcast_to(hits.reshape(slots, rows, 1), (slots, rows, BLK))
 
+    held = placed[:, :, None, :] & in_row
+    held = held[..., None] & (ids % LBLK_DEV == jnp.arange(LBLK_DEV)[:, None, None]).transpose(1, 2, 0)[
+        :, None, None
+    ]
+    number = jnp.arange(slots).reshape(n_mp, cap, 1, 1, 1)
+    where = slots - jnp.sum(jnp.where(held, slots - number, 0), axis=(1, 3))
+    where = where.reshape(blocks, LBLK_DEV).astype(jnp.int32)
+
     small = (TB, BLK)
     wide = (rows, TB, feat)
-    lat, pg, err_all, errors = pl.pallas_call(
+    pg, stream_wide, grad_dec, errors = pl.pallas_call(
         functools.partial(main_kernel, n_mp, n_dp, rows, cap),
         out_shape=(
-            shape((slots,) + small, BF16),
-            shape((slots,) + small, BF16),
-            shape((blocks, TB, feat), BF16),
-            shape(wide, BF16),
-        ),
-        in_specs=[smem] + [vmem] * 6,
+            shape((slots + 1,) + small, BF16),
+            shape((feat, blocks * TB), BF16),
+            shape((feat, LBLK_DEV * BLK), BF16),
+            shape((feat, tok_count), BF16),
+        ),
+        in_specs=[smem] * 2 + [vmem] * 6,
         out_specs=(vmem,) * 4,
         scratch_shapes=[
-            pltpu.VMEM((slots,) + small, BF16),
-            pltpu.VMEM((slots,) + small, BF16),
+            pltpu.VMEM((slots + 1,) + small, BF16),
+            pltpu.VMEM((slots + 1,) + small, BF16),
             pltpu.VMEM((blocks, TB, feat), BF16),
             pltpu.VMEM((tok_count, cap * BLK), BF16),
             pltpu.VMEM((cap * BLK, feat), BF16),
+            pltpu.VMEM((feat, blocks * TB), BF16),
+            pltpu.VMEM((blocks * TB, 2 * BLK), BF16),
         ]
         + [pltpu.VMEM((dps, per) + small, F32)] * 5
         + [pltpu.VMEM((mps,) + wide, t) for t in (BF16, F32, BF16, BF16, BF16)]
@@ -348,35 +370,31 @@
         ),
     )(
         table,
+        where,
         hits,
         stream_all,
         enc_blocks,
-        dec_weight.reshape(LBLK_DEV, BLK, feat),
+        dec_blocks,
         enc_bias.reshape(LBLK_DEV, 1, BLK),
         dec_bias.reshape(1, feat),
     )
 
-    grad_enc, grad_bias, grad_dec = pl.pallas_call(
-        functools.partial(grad_kernel, slots),
+    grad_enc, grad_bias = pl.pallas_call(
+        functools.partial(grad_kernel, blocks),
+        grid=(LBLK_DEV // 2,),
         out_shape=(
             shape((feat, LBLK_DEV * BLK), BF16),
-            shape((LBLK_DEV, BLK), F32),
-            shape((LBLK_DEV, BLK, feat), BF16),
-        ),
-        in_specs=[smem] + [vmem] * 4,
-        out_specs=(vmem,) * 3,
-        scratch_shapes=[
-            pltpu.VMEM((LBLK_DEV, feat, BLK), F32),
-            pltpu.VMEM((LBLK_DEV, BLK, feat), F32),
-        ],
+            shape((1, LBLK_DEV * BLK), F32),
+        ),
+        in_specs=[smem] + [vmem] * 2,
+        out_specs=(
+            pl.BlockSpec((feat, 2 * BLK), lambda i: (0, i)),
+            pl.BlockSpec((1, 2 * BLK), lambda i: (0, i)),
+        ),
+        scratch_shapes=[pltpu.VMEM((blocks * TB, 2 * BLK), BF16)],
         compiler_params=pltpu.CompilerParams(vmem_limit_bytes=VMEM_BYTES),
-    )(table, stream_all, err_all, lat, pg)
-    return (
-        grad_enc,
-        grad_bias.reshape(LBLK_DEV * BLK),
-        grad_dec.reshape(LBLK_DEV * BLK, feat),
-        errors.reshape(tok_count, feat),
-    )
+    )(where, stream_wide, pg)
+    return (grad_enc, grad_bias.reshape(LBLK_DEV * BLK), grad_dec.T, errors.T)
 
 
 def solution(mesh):

time: 164 us -> 155 us (0.945)
  local copies, waits for them, and re-layouts: 14.1 us -> 8.42 us
  Pallas kernels: 146 us -> 142 us
    pallas_call x1, Pallas kernels: 13 us -> 6.2 us  [local(): pl.pallas_call(functools.partial(grad_kernel, blocks), grid=(LBLK_DEV //...]
    unnamed x8, local copies, waits for them, and re-layouts: 12.1 us -> 6.44 us
    pallas_call x1, Pallas kernels: 14.6 us -> 16.7 us  [local(): pl.pallas_call(functools.partial(gather_kernel, n_mp, rows), out_shape=(s...]
where the time goes in v2:
time: 155 us; the launch traced here: 153 us
  Pallas kernels  142 us (92%)
  local copies, waits for them, and re-layouts  8.42 us (5%)
    pallas_call x1, Pallas kernels, local(): pl.pallas_call(functools.partial(main_kernel, n_mp, n_dp, rows, cap), out...  120 us
    pallas_call x1, Pallas kernels, local(): pl.pallas_call(functools.partial(gather_kernel, n_mp, rows), out_shape=(s...  16.7 us
    unnamed x8, local copies, waits for them, and re-layouts  6.44 us
    pallas_call x1, Pallas kernels, local(): pl.pallas_call(functools.partial(grad_kernel, blocks), grid=(LBLK_DEV //...  6.2 us

profile of v2, /device:TPU:0, one launch (start us, length us, event | category | flops | bytes accessed | tf_op | source)
XLA Modules:
  0.0 152.6 jit_solution(13252364243779315306)
XLA Ops:
  0.7 0.1 add.55
  0.7 0.1 add.56
  0.8 0.7 reshape.255.dec_bias
  1.5 0.7 scatter.4.list_ref
  2.2 0.0 copy-start.1
  2.2 1.0 copy-done.1
  3.2 0.0 copy-start.2
  3.2 16.7 %shard_map.93 = (bf16[8,128,576]{2,1,0:T(8,128)(2,1)S(1)}, s32[4,8,128]{2,1,0:T(8,128)S(1)}, bf16[16,576,128]{2,1,0:T(8,128)(2,1)S(1)}, bf16[16,128,576]{2,1,0:T(8,128)(2,1)}) custom-call(bf16[576,256]{1,0:T(8,128)(2,1)S(1)} %bitcast.11, s32[1,8,128]{2,1,0:T(8,128)S(1)} %scatter.4.list_ref, bf16[576,2048]{1,0:T(8,128)(2,1)} %enc_ref.1, ...), custom_call_target="tpu_custom_call" | custom-call | tf_op jit(solution)/shard_map/pallas_call | solution.py:302
  19.9 0.0 copy-start
  19.9 1.4 copy-done
  21.3 0.1 reshape.250
  21.4 0.1 convert_reduce_fusion.1
  21.6 0.2 select_reduce_fusion.2
  21.8 0.1 reduce_sum.50
  21.9 0.1 stack.7
  22.0 0.1 convert_reduce_fusion
  22.1 0.1 iota_compare_fusion
  22.2 0.3 select_reduce_fusion
  22.5 0.1 copy.14
  22.6 0.1 broadcast_in_dim.36.hits
  22.7 0.0 copy-done.2
  22.7 119.6 %shard_map.94 = (bf16[33,128,128]{2,1,0:T(8,128)(2,1)S(1)}, bf16[576,1024]{1,0:T(8,128)(2,1)S(1)}, bf16[576,2048]{1,0:T(8,128)(2,1)}, bf16[576,256]{1,0:T(8,128)(2,1)S(1)}) custom-call(s32[2,32]{1,0:T(2,128)S(1)} %pad_add_fusion.table, s32[8,16]{1,0:T(8,128)S(1)} %bitcast.13, f32[32,2,128]{2,1,0:T(2,128)S(1)} %broadcast_in_dim.36.hits, ...), custom_call_target="tpu_custom_call" | custom-call | tf_op jit(solution)/shard_map/pallas_call | solution.py:345
  142.3 6.2 %shard_map.95 = (bf16[576,2048]{1,0:T(8,128)(2,1)}, f32[1,2048]{1,0:T(1,128)}) custom-call(s32[8,16]{1,0:T(8,128)S(1)} %bitcast.14, bf16[576,1024]{1,0:T(8,128)(2,1)S(1)} %get-tuple-element.30.stream, bf16[33,128,128]{2,1,0:T(8,128)(2,1)S(1)} %get-tuple-element.31.pg), custom_call_target="tpu_custom_call" | custom-call | tf_op jit(solution)/shard_map/pallas_call | solution.py:382
  148.5 3.4 %copy.18 = bf16[2048,576]{0,1:T(8,128)(2,1)} copy(bf16[2048,576]{0,1:T(8,128)(2,1)} %bitcast.17) | data formatting | bytes 4718592
  151.8 0.7 copy.19
  (14 shorter events, 0.1 us)
Async XLA Ops:
  2.2 1.0 copy-start.1
  3.2 19.5 %copy-start.2 = (f32[2048]{0:T(1024)S(1)}, f32[2048]{0:T(1024)}, u32[]{:S(2)}) copy-start(f32[2048]{0:T(1024)} %param.11) | copy-start | bytes 24580
  19.9 1.4 copy-start

commit v3 on v2

v3 whole, which is shorter than its diff:
```python
import functools

import jax
import jax.numpy as jnp
from jax import lax
from jax.experimental import pallas as pl
from jax.experimental.pallas import tpu as pltpu
from jax.sharding import PartitionSpec as P

BLK = 128
TB = 128
LIST = 8
LBLK_DEV = 16
F32 = jnp.float32
BF16 = jnp.bfloat16
VMEM_BYTES = 48 * 1024 * 1024


class Axis:
    def __init__(self, name, size):
        self.name = name
        self.fars = size // 2
        self.me = lax.axis_index(name)
        self.far = self.me // 2
        self.near = self.me % 2

    def later(self, step):
        return lax.rem(self.far + step, self.fars)

    def index(self, far, near):
        return 2 * far + near

    def sibling(self):
        return self.index(self.far, 1 - self.near)

    def push(self, src, dst, send, recv, target):
        return pltpu.make_async_remote_copy(
            src_ref=src,
            dst_ref=dst,
            send_sem=send,
            recv_sem=recv,
            device_id={self.name: target},
            device_id_type=pl.DeviceIdType.MESH,
        )

    def greet(self, barrier):
        pl.semaphore_signal(
            barrier, inc=1, device_id={self.name: self.sibling()}, device_id_type=pl.DeviceIdType.MESH
        )
        for step in range(1, self.fars):
            pl.semaphore_signal(
                barrier,
                inc=1,
                device_id={self.name: self.index(self.later(step), self.near)},
                device_id_type=pl.DeviceIdType.MESH,
            )
        return self.fars


def gather_start(ax, buf, region, sems, pending):
    far_send, far_recv, near_send, near_recv = sems
    mine = buf.at[region(ax.me)]
    copies = []
    for step in range(1, ax.fars):
        peer = ax.later(step)
        copies.append(
            ax.push(mine, mine, far_send.at[peer], far_recv.at[ax.far], ax.index(peer, ax.near))
        )
    copies.append(ax.push(mine, mine, near_send.at[ax.far], near_recv.at[ax.far], ax.sibling()))
    for copy in copies:
        copy.start()
    pending.extend(copies)


def gather_finish(ax, buf, region, sems, pending, work=lambda step: None):
    far_send, far_recv, near_send, near_recv = sems
    work(0)
    for step in range(1, ax.fars):
        peer = ax.later(ax.fars - step)
        landed = buf.at[region(ax.index(peer, ax.near))]
        ax.push(
            landed, landed, far_send.at[peer], far_recv.at[peer], ax.index(peer, ax.near)
        ).wait_recv()
        copy = ax.push(landed, landed, near_send.at[peer], near_recv.at[peer], ax.sibling())
        copy.start()
        pending.append(copy)
        work(step)
    for step in range(ax.fars):
        peer = ax.later(ax.fars - step)
        landed = buf.at[region(ax.index(peer, 1 - ax.near))]
        ax.push(
            landed, landed, near_send.at[peer], near_recv.at[peer], ax.sibling()
        ).wait_recv()


def scatter_sum(ax, produce, bufs, sems, pending):
    away, own, near_in, pair, far_in = bufs
    far_send, far_recv, near_send, near_recv = sems
    for step in range(1, ax.fars + 1):
        peer = ax.later(step)
        produce(ax.index(peer, 1 - ax.near), away, peer)
        copy = ax.push(
            away.at[peer], near_in.at[peer], near_send.at[peer], near_recv.at[peer], ax.sibling()
        )
        copy.start()
        pending.append(copy)
    yield

    def wait_near(peer):
        ax.push(
            near_in.at[peer], near_in.at[peer], near_send.at[peer], near_recv.at[peer], ax.sibling()
        ).wait_recv()

    for step in range(1, ax.fars):
        peer = ax.later(step)
        produce(ax.index(peer, ax.near), own, peer)
        wait_near(peer)
        pair[peer] = (own[peer] + near_in[peer].astype(F32)).astype(pair.dtype)
        copy = ax.push(
            pair.at[peer],
            far_in.at[ax.far],
            far_send.at[peer],
            far_recv.at[ax.far],
            ax.index(peer, ax.near),
        )
        copy.start()
        pending.append(copy)
    produce(ax.me, own, ax.far)
    yield
    wait_near(ax.far)
    total = own[ax.far] + near_in[ax.far].astype(F32)
    for step in range(1, ax.fars):
        peer = ax.later(ax.fars - step)
        ax.push(
            far_in.at[peer],
            far_in.at[peer],
            far_send.at[peer],
            far_recv.at[peer],
            ax.index(peer, ax.near),
        ).wait_recv()
        total = total + far_in[peer].astype(F32)
    yield total


def gather_kernel(
    n_mp, rows, stream_ref, list_ref, enc_ref,
    stream_out, list_out, enc_out, buf, lists, *sems
):
    ax = Axis("mp", n_mp)
    barrier = pltpu.get_barrier_semaphore()
    greeted = ax.greet(barrier)
    for j in range(rows):
        buf[ax.me * rows + j] = stream_ref[:, j * TB:(j + 1) * TB].T
    pl.semaphore_wait(barrier, greeted)
    lists[pl.ds(ax.me, 1)] = list_ref[...]
    pending = []

    def one_list(m):
        return pl.ds(m, 1)

    def home(m):
        return pl.ds(m * rows, rows)

    gather_start(ax, lists, one_list, sems[4:8], pending)
    gather_start(ax, buf, home, sems[0:4], pending)
    for k in range(LBLK_DEV):
        enc_out[k] = enc_ref[:, k * BLK:(k + 1) * BLK]
    gather_finish(ax, lists, one_list, sems[4:8], pending)
    gather_finish(ax, buf, home, sems[0:4], pending)
    for copy in pending:
        copy.wait_send()
    stream_out[...] = buf[...]
    list_out[...] = lists[...]


def spread_pair(blocks, pair, where, held, spread):
    for b in range(blocks):
        for i in range(2):
            spread[b * TB:(b + 1) * TB, i * BLK:(i + 1) * BLK] = held[where[b, 2 * pair + i]]


def main_kernel(
    n_mp, n_dp, rows, cap, parts,
    table, where, hits, stream, enc, dec_in, enc_bias, dec_bias,
    pg_out, stream_out, gdec_out, err_out,
    lat, pg, err, dec, dec_wide, picked, picked_dec, err_wide, spread, *rest,
):
    mp = Axis("mp", n_mp)
    dp = Axis("dp", n_dp)
    per = n_mp * cap // n_dp
    part = per // parts
    blocks = n_mp * rows
    pre_bufs, dec_bufs, code_bufs, sems = rest[0:5], rest[5:10], rest[10:15], rest[15:]
    barrier = pltpu.get_barrier_semaphore()
    count = mp.greet(barrier) + dp.greet(barrier)
    empty = jnp.zeros((TB, BLK), BF16)
    lat[n_mp * cap] = empty
    pg[n_mp * cap] = empty
    pl.semaphore_wait(barrier, count)
    pending = []

    def group(i):
        return sems[4 * i:4 * i + 4]

    def home_rows(m):
        return pl.ds(m * rows, rows)

    def region(p):
        return lambda m: pl.ds(m * per + p * part, part)

    def producer(p, left, right):
        def produce(chunk, dest, place):
            def one(i, _):
                slot = chunk * per + p * part + i
                dest[place, i] = jnp.dot(
                    left[table[0, slot]], right[table[1, slot]], preferred_element_type=F32
                ).astype(dest.dtype)
                return 0

            lax.fori_loop(0, part, one, 0, unroll=True)

        return produce

    def reduce_and_gather(left, right, bufs, first, held, finish, aside, work):
        sums = [
            scatter_sum(
                dp,
                producer(p, left, right),
                [b.at[p] for b in bufs],
                group(first + p),
                pending,
            )
            for p in range(parts)
        ]
        for p in range(parts):
            next(sums[p])
        for p in range(parts):
            next(sums[p])
            aside(p)
        for p in range(parts):
            total = next(sums[p])
            for i in range(part):
                slot = dp.me * per + p * part + i
                held[slot] = finish(slot, total[i])
            gather_start(dp, held, region(p), group(first + parts + p), pending)
        for p in range(parts):
            gather_finish(
                dp, held, region(p), group(first + parts + p), pending, functools.partial(work, p)
            )

    def activate(slot, pre_sum):
        shifted = pre_sum + enc_bias[table[1, slot]]
        live = jnp.sum(hits[slot], axis=0, keepdims=True)
        return (jnp.maximum(shifted, 0.0) * live).astype(BF16)

    def turn_dec(p):
        for k in range(p * LBLK_DEV // parts, (p + 1) * LBLK_DEV // parts):
            dec[k] = dec_in[:, k * BLK:(k + 1) * BLK].T

    def split_dec(p, step):
        calls = parts * dp.fars
        at = p * dp.fars + step
        for k in range(at * LBLK_DEV // calls, (at + 1) * LBLK_DEV // calls):
            dec_wide[k] = dec_in[:, k * BLK:(k + 1) * BLK]

    reduce_and_gather(stream, enc, pre_bufs, 0, lat, activate, turn_dec, split_dec)

    def produce_dec(home, dest, place):
        for c in range(cap):
            slot = home * cap + c
            picked_dec[c * BLK:(c + 1) * BLK, :] = dec[table[1, slot]]
            block = lat[slot]
            for j in range(rows):
                hit = jnp.broadcast_to(hits[slot, j:j + 1], (TB, BLK)).astype(BF16)
                picked[j * TB:(j + 1) * TB, c * BLK:(c + 1) * BLK] = block * hit
        out = jnp.dot(picked[...], picked_dec[...], preferred_element_type=F32)
        dest[place] = out.reshape(dest.shape[1:]).astype(dest.dtype)

    sums = scatter_sum(mp, produce_dec, dec_bufs, group(4 * parts), pending)
    next(sums)
    next(sums)
    recon = next(sums) + dec_bias[...][None]
    mine = (recon - stream[home_rows(mp.me)].astype(F32)).astype(BF16)
    err[home_rows(mp.me)] = mine
    gather_start(mp, err, home_rows, group(4 * parts + 1), pending)
    for j in range(rows):
        err_out[:, j * TB:(j + 1) * TB] = mine[j].T
    for b in range(blocks):
        stream_out[:, b * TB:(b + 1) * TB] = stream[b].T
    gather_finish(mp, err, home_rows, group(4 * parts + 1), pending)

    def to_pre_grad(slot, code):
        on = lat[slot].astype(F32) > 0
        return jnp.where(on, code * (1.0 / TB), 0.0).astype(BF16)

    def turn_err(p):
        for b in range(p * blocks // parts, (p + 1) * blocks // parts):
            err_wide[:, b * TB:(b + 1) * TB] = err[b].T

    def grad_dec(p, step):
        calls = parts * dp.fars
        at = p * dp.fars + step
        pairs = LBLK_DEV // 2

        def one(pair, _):
            spread_pair(blocks, pair, where, lat, spread)
            total = jnp.dot(err_wide[...], spread[...], preferred_element_type=F32)
            lane = pl.multiple_of(pair * 2 * BLK, 2 * BLK)
            gdec_out[:, pl.ds(lane, 2 * BLK)] = (total * (1.0 / TB)).astype(BF16)
            return 0

        if at * pairs // calls < (at + 1) * pairs // calls:
            lax.fori_loop(at * pairs // calls, (at + 1) * pairs // calls, one, 0)

    reduce_and_gather(err, dec_wide, code_bufs, 2 * parts, pg, to_pre_grad, turn_err, grad_dec)
    pg_out[...] = pg[...]
    for copy in pending:
        copy.wait_send()


def grad_kernel(blocks, where, stream, pg, gdec_in, err_in, genc, gbias, gdec, err, spread):
    gdec[...] = gdec_in[...]

    @pl.when(pl.program_id(0) == 0)
    def _():
        err[...] = err_in[...]

    spread_pair(blocks, pl.program_id(0), where, pg, spread)
    genc[...] = jnp.dot(stream[...], spread[...], preferred_element_type=F32).astype(BF16)
    gbias[...] = jnp.sum(spread[...].astype(F32), axis=0, keepdims=True)


def local(n_mp, n_dp, stream, active_lists, enc_weight, enc_bias, dec_weight, dec_bias):
    tok_count, feat = stream.shape
    rows = tok_count // TB
    cap = max(2, 16 * rows // n_mp)
    slots = n_mp * cap
    per = slots // n_dp
    parts = 2 if per % 2 == 0 else 1
    chunk = (parts, n_dp // 2, per // parts, TB, BLK)
    blocks = n_mp * rows
    mps, dps = n_mp // 2, n_dp // 2
    vmem = pl.BlockSpec(memory_space=pltpu.VMEM)
    smem = pl.BlockSpec(memory_space=pltpu.SMEM)
    dma = pltpu.SemaphoreType.DMA
    shape = jax.ShapeDtypeStruct

    lists = jnp.full((1, 8, 128), -1, jnp.int32).at[0, :rows, :LIST].set(active_lists)
    stream_all, lists_all, enc_blocks = pl.pallas_call(
        functools.partial(gather_kernel, n_mp, rows),
        out_shape=(
            shape((blocks, TB, feat), BF16),
            shape((n_mp, 8, 128), jnp.int32),
            shape((LBLK_DEV, feat, BLK), BF16),
        ),
        in_specs=[vmem] * 3,
        out_specs=(vmem,) * 3,
        scratch_shapes=[
            pltpu.VMEM((blocks, TB, feat), BF16),
            pltpu.VMEM((n_mp, 8, 128), jnp.int32),
        ] + [dma((mps,))] * 8,
        compiler_params=pltpu.CompilerParams(
            collective_id=0, has_side_effects=True, vmem_limit_bytes=VMEM_BYTES
        ),
    )(stream.T, lists, enc_weight)

    ids = lists_all[:, :rows, :LIST].reshape(n_mp, rows * LIST)
    entry = jnp.arange(rows * LIST)
    mine = (ids >= 0) & (ids // LBLK_DEV == lax.axis_index("mp"))
    before = jnp.sum(mine[:, None, :] & (entry[None, :] < entry[:, None])[None], axis=2)
    placed = mine[:, None, :] & (before[:, None, :] == jnp.arange(cap)[None, :, None])
    home = jnp.arange(n_mp)[:, None, None] * rows
    table = jnp.stack([
        jnp.sum(jnp.where(placed, entry // LIST, 0), axis=2) + home[:, :, 0],
        jnp.sum(jnp.where(placed, (ids % LBLK_DEV)[:, None, :], 0), axis=2),
    ]).reshape(2, slots).astype(jnp.int32)
    in_row = (entry // LIST)[None, :] == jnp.arange(rows)[:, None]
    hits = jnp.sum((placed[:, :, None, :] & in_row).astype(F32), axis=3)
    hits = jnp.broadcast_to(hits.reshape(slots, rows, 1), (slots, rows, BLK))

    held = placed[:, :, None, :] & in_row
    held = held[..., None] & (ids % LBLK_DEV == jnp.arange(LBLK_DEV)[:, None, None]).transpose(1, 2, 0)[
        :, None, None
    ]
    number = jnp.arange(slots).reshape(n_mp, cap, 1, 1, 1)
    where = slots - jnp.sum(jnp.where(held, slots - number, 0), axis=(1, 3))
    where = where.reshape(blocks, LBLK_DEV).astype(jnp.int32)

    small = (TB, BLK)
    wide = (rows, TB, feat)
    pg, stream_wide, grad_dec, errors = pl.pallas_call(
        functools.partial(main_kernel, n_mp, n_dp, rows, cap, parts),
        out_shape=(
            shape((slots + 1,) + small, BF16),
            shape((feat, blocks * TB), BF16),
            shape((feat, LBLK_DEV * BLK), BF16),
            shape((feat, tok_count), BF16),
        ),
        in_specs=[smem] * 2 + [vmem] * 6,
        out_specs=(vmem,) * 4,
        scratch_shapes=[
            pltpu.VMEM((slots + 1,) + small, BF16),
            pltpu.VMEM((slots + 1,) + small, BF16),
            pltpu.VMEM((blocks, TB, feat), BF16),
            pltpu.VMEM((LBLK_DEV, BLK, feat), BF16),
            pltpu.VMEM((LBLK_DEV, feat, BLK), BF16),
            pltpu.VMEM((tok_count, cap * BLK), BF16),
            pltpu.VMEM((cap * BLK, feat), BF16),
            pltpu.VMEM((feat, blocks * TB), BF16),
            pltpu.VMEM((blocks * TB, 2 * BLK), BF16),
        ]
        + [pltpu.VMEM(chunk, F32)] * 5
        + [pltpu.VMEM((mps,) + wide, t) for t in (BF16, F32, BF16, BF16, BF16)]
        + [pltpu.VMEM(chunk, t) for t in (BF16, F32, BF16, BF16, BF16)]
        + [dma((dps,))] * (16 * parts) + [dma((mps,))] * 8,
        compiler_params=pltpu.CompilerParams(
            collective_id=1, has_side_effects=True, vmem_limit_bytes=VMEM_BYTES
        ),
    )(
        table,
        where,
        hits,
        stream_all,
        enc_blocks,
        dec_weight.T,
        enc_bias.reshape(LBLK_DEV, 1, BLK),
        dec_bias.reshape(1, feat),
    )

    pair = pl.BlockSpec((feat, 2 * BLK), lambda i: (0, i))
    whole = pl.BlockSpec((feat, tok_count), lambda i: (0, 0))
    grad_enc, grad_bias, grad_dec, errors = pl.pallas_call(
        functools.partial(grad_kernel, blocks),
        grid=(LBLK_DEV // 2,),
        out_shape=(
            shape((feat, LBLK_DEV * BLK), BF16),
            shape((1, LBLK_DEV * BLK), F32),
            shape((feat, LBLK_DEV * BLK), BF16),
            shape((feat, tok_count), BF16),
        ),
        in_specs=[smem] + [vmem] * 2 + [pair, whole],
        out_specs=(pair, pl.BlockSpec((1, 2 * BLK), lambda i: (0, i)), pair, whole),
        scratch_shapes=[pltpu.VMEM((blocks * TB, 2 * BLK), BF16)],
        compiler_params=pltpu.CompilerParams(vmem_limit_bytes=VMEM_BYTES),
    )(where, stream_wide, pg, grad_dec, errors)
    return (grad_enc, grad_bias.reshape(LBLK_DEV * BLK), grad_dec.T, errors.T)


def solution(mesh):
    return jax.shard_map(
        functools.partial(local, mesh.shape["mp"], mesh.shape["dp"]),
        mesh=mesh,
        in_specs=(
            P(("groups", "mp"), "dp"),
            P(("groups", "mp"), None),
            P("dp", "mp"),
            P("mp"),
            P("mp", "dp"),
            P("dp"),
        ),
        out_specs=(
            P(("groups", "dp"), "mp"),
            P(("groups", "mp")),
            P(("groups", "mp"), "dp"),
            P(("groups", "mp"), "dp"),
        ),
        check_vma=False,
    )
```

time: 155 us -> 143 us (0.923); the launches traced: 153 us -> 143 us
  Pallas kernels: 142 us -> 135 us
  local copies, waits for them, and re-layouts: 8.42 us -> 6.01 us
    pallas_call x1, Pallas kernels: 120 us -> 114 us  [local(): pl.pallas_call(functools.partial(main_kernel, n_mp, n_dp, rows, cap, part...]
    unnamed x8, local copies, waits for them, and re-layouts: 6.44 us -> 4.02 us
    pallas_call x1, Pallas kernels: 16.7 us -> 14.6 us  [local(): pl.pallas_call(functools.partial(gather_kernel, n_mp, rows), out_shape=(s...]
where the time goes in v3:
time: 143 us
  Pallas kernels  135 us (94%)
  local copies, waits for them, and re-layouts  6.01 us (4%)
    pallas_call x1, Pallas kernels, local(): pl.pallas_call(functools.partial(main_kernel, n_mp, n_dp, rows, cap, part...  114 us
    pallas_call x1, Pallas kernels, local(): pl.pallas_call(functools.partial(gather_kernel, n_mp, rows), out_shape=(s...  14.6 us
    pallas_call x1, Pallas kernels, local(): pl.pallas_call(functools.partial(grad_kernel, blocks), grid=(LBLK_DEV //...  6.6 us
    unnamed x8, local copies, waits for them, and re-layouts  4.02 us

profile of v3, /device:TPU:0, one launch (start us, length us, event | category | flops | bytes accessed | tf_op | source)
XLA Modules:
  0.0 143.0 jit_solution(2567829839684059830)
XLA Ops:
  0.6 0.0 copy-start.3
  0.7 0.1 add.55
  0.7 0.1 add.56
  0.8 0.7 reshape.255.dec_bias
  1.5 0.7 scatter.4.list_ref
  2.2 0.0 copy-start.2
  2.2 1.0 copy-done.2
  3.2 14.6 %shard_map.93 = (bf16[8,128,576]{2,1,0:T(8,128)(2,1)S(1)}, s32[4,8,128]{2,1,0:T(8,128)S(1)}, bf16[16,576,128]{2,1,0:T(8,128)(2,1)S(1)}) custom-call(bf16[576,256]{1,0:T(8,128)(2,1)S(1)} %bitcast.11, s32[1,8,128]{2,1,0:T(8,128)S(1)} %scatter.4.list_ref, bf16[576,2048]{1,0:T(8,128)(2,1)} %enc_ref.1), custom_call_target="tpu_custom_call" | custom-call | tf_op jit(solution)/shard_map/pallas_call | solution.py:349
  17.8 0.0 copy-start.1
  17.8 1.4 copy-done.1
  19.2 0.1 reshape.250
  19.3 0.1 convert_reduce_fusion.1
  19.4 0.2 select_reduce_fusion.2
  19.7 0.1 reduce_sum.50
  19.8 0.1 stack.7
  19.9 0.1 convert_reduce_fusion
  20.0 0.1 iota_compare_fusion
  20.1 0.3 select_reduce_fusion
  20.4 0.1 copy.14
  20.5 0.1 broadcast_in_dim.36.hits
  20.5 0.0 copy-done.3
  20.6 114.2 %shard_map.94 = (bf16[33,128,128]{2,1,0:T(8,128)(2,1)S(1)}, bf16[576,1024]{1,0:T(8,128)(2,1)S(1)}, bf16[576,2048]{1,0:T(8,128)(2,1)}, bf16[576,256]{1,0:T(8,128)(2,1)S(1)}) custom-call(s32[2,32]{1,0:T(2,128)S(1)} %pad_add_fusion.table, s32[8,16]{1,0:T(8,128)S(1)} %bitcast.12, f32[32,2,128]{2,1,0:T(2,128)S(1)} %broadcast_in_dim.36.hits, ...), custom_call_target="tpu_custom_call" | custom-call | tf_op jit(solution)/shard_map/pallas_call | solution.py:391
  134.8 0.0 copy-start
  134.8 1.7 %copy-done = bf16[576,2048]{1,0:T(8,128)(2,1)S(1)} copy-done((bf16[576,2048]{1,0:T(8,128)(2,1)S(1)}, bf16[576,2048]{1,0:T(8,128)(2,1)}, u32[]{:S(2)}) %copy-start) | copy-done | bytes 2359320
  136.4 6.6 %shard_map.95 = (bf16[576,2048]{1,0:T(8,128)(2,1)}, f32[1,2048]{1,0:T(1,128)}, bf16[576,2048]{1,0:T(8,128)(2,1)}, bf16[576,256]{1,0:T(8,128)(2,1)}) custom-call(s32[8,16]{1,0:T(8,128)S(1)} %bitcast.13, bf16[576,1024]{1,0:T(8,128)(2,1)S(1)} %get-tuple-element.30.stream, bf16[33,128,128]{2,1,0:T(8,128)(2,1)S(1)} %get-tuple-element.31.pg, ...), custom_call_target="tpu_custom_call" | custom-call | tf_op jit(solution)/shard_map/pallas_call | solution.py:432
  (14 shorter events, 0.1 us)
Async XLA Ops:
  0.6 19.9 %copy-start.3 = (f32[2048]{0:T(1024)S(1)}, f32[2048]{0:T(1024)}, u32[]{:S(2)}) copy-start(f32[2048]{0:T(1024)} %param.11) | copy-start | bytes 24580
  2.2 1.0 copy-start.2
  17.8 1.4 copy-start.1
  134.8 1.7 %copy-start = (bf16[576,2048]{1,0:T(8,128)(2,1)S(1)}, bf16[576,2048]{1,0:T(8,128)(2,1)}, u32[]{:S(2)}) copy-start(bf16[576,2048]{1,0:T(8,128)(2,1)} %get-tuple-element.32.gdec_in) | copy-start | bytes 7077892

commit v4 on v3

--- a/solution.py
+++ b/solution.py
@@ -72,7 +72,7 @@
     pending.extend(copies)
 
 
-def gather_finish(ax, buf, region, sems, pending, work=lambda step: None):
+def gather_forward(ax, buf, region, sems, pending, work=lambda step: None):
     far_send, far_recv, near_send, near_recv = sems
     work(0)
     for step in range(1, ax.fars):
@@ -85,6 +85,10 @@
         copy.start()
         pending.append(copy)
         work(step)
+
+
+def gather_finish(ax, buf, region, sems):
+    far_send, far_recv, near_send, near_recv = sems
     for step in range(ax.fars):
         peer = ax.later(ax.fars - step)
         landed = buf.at[region(ax.index(peer, 1 - ax.near))]
@@ -104,7 +108,7 @@
         )
         copy.start()
         pending.append(copy)
-    yield
+        yield
 
     def wait_near(peer):
         ax.push(
@@ -125,6 +129,7 @@
         )
         copy.start()
         pending.append(copy)
+        yield
     produce(ax.me, own, ax.far)
     yield
     wait_near(ax.far)
@@ -165,8 +170,10 @@
     gather_start(ax, buf, home, sems[0:4], pending)
     for k in range(LBLK_DEV):
         enc_out[k] = enc_ref[:, k * BLK:(k + 1) * BLK]
-    gather_finish(ax, lists, one_list, sems[4:8], pending)
-    gather_finish(ax, buf, home, sems[0:4], pending)
+    gather_forward(ax, lists, one_list, sems[4:8], pending)
+    gather_forward(ax, buf, home, sems[0:4], pending)
+    gather_finish(ax, lists, one_list, sems[4:8])
+    gather_finish(ax, buf, home, sems[0:4])
     for copy in pending:
         copy.wait_send()
     stream_out[...] = buf[...]
@@ -232,21 +239,28 @@
             )
             for p in range(parts)
         ]
+        for _ in range(dp.fars):
+            next(sums[0])
         for p in range(parts):
-            next(sums[p])
-        for p in range(parts):
-            next(sums[p])
-            aside(p)
+            for _ in range(dp.fars):
+                if p + 1 < parts:
+                    next(sums[p + 1])
+                next(sums[p])
+        aside(0)
         for p in range(parts):
             total = next(sums[p])
             for i in range(part):
                 slot = dp.me * per + p * part + i
                 held[slot] = finish(slot, total[i])
             gather_start(dp, held, region(p), group(first + parts + p), pending)
+            if p + 1 < parts:
+                aside(p + 1)
         for p in range(parts):
-            gather_finish(
+            gather_forward(
                 dp, held, region(p), group(first + parts + p), pending, functools.partial(work, p)
             )
+        for p in range(parts):
+            gather_finish(dp, held, region(p), group(first + parts + p))
 
     def activate(slot, pre_sum):
         shifted = pre_sum + enc_bias[table[1, slot]]
@@ -277,8 +291,8 @@
         dest[place] = out.reshape(dest.shape[1:]).astype(dest.dtype)
 
     sums = scatter_sum(mp, produce_dec, dec_bufs, group(4 * parts), pending)
-    next(sums)
-    next(sums)
+    for _ in range(2 * mp.fars):
+        next(sums)
     recon = next(sums) + dec_bias[...][None]
     mine = (recon - stream[home_rows(mp.me)].astype(F32)).astype(BF16)
     err[home_rows(mp.me)] = mine
@@ -287,7 +301,8 @@
         err_out[:, j * TB:(j + 1) * TB] = mine[j].T
     for b in range(blocks):
         stream_out[:, b * TB:(b + 1) * TB] = stream[b].T
-    gather_finish(mp, err, home_rows, group(4 * parts + 1), pending)
+    gather_forward(mp, err, home_rows, group(4 * parts + 1), pending)
+    gather_finish(mp, err, home_rows, group(4 * parts + 1))
 
     def to_pre_grad(slot, code):
         on = lat[slot].astype(F32) > 0

time: 143 us -> 139 us (0.972)
  Pallas kernels: 135 us -> 131 us
    pallas_call x1, Pallas kernels: 114 us -> 110 us  [local(): pl.pallas_call(functools.partial(main_kernel, n_mp, n_dp, rows, cap, part...]
where the time goes in v4:
time: 139 us
  Pallas kernels  131 us (94%)
  local copies, waits for them, and re-layouts  6.01 us (4%)
    pallas_call x1, Pallas kernels, local(): pl.pallas_call(functools.partial(main_kernel, n_mp, n_dp, rows, cap, part...  110 us
    pallas_call x1, Pallas kernels, local(): pl.pallas_call(functools.partial(gather_kernel, n_mp, rows), out_shape=(s...  14.6 us
    pallas_call x1, Pallas kernels, local(): pl.pallas_call(functools.partial(grad_kernel, blocks), grid=(LBLK_DEV //...  6.59 us
    unnamed x8, local copies, waits for them, and re-layouts  4.02 us

profile of v4, /device:TPU:0, one launch (start us, length us, event | category | flops | bytes accessed | tf_op | source)
XLA Modules:
  0.0 138.9 jit_solution(8810310603031503354)
XLA Ops:
  0.6 0.0 copy-start.3
  0.7 0.1 add.55
  0.7 0.1 add.56
  0.8 0.7 reshape.255.dec_bias
  1.5 0.7 scatter.4.list_ref
  2.2 0.0 copy-start.2
  2.2 1.0 copy-done.2
  3.2 14.6 %shard_map.93 = (bf16[8,128,576]{2,1,0:T(8,128)(2,1)S(1)}, s32[4,8,128]{2,1,0:T(8,128)S(1)}, bf16[16,576,128]{2,1,0:T(8,128)(2,1)S(1)}) custom-call(bf16[576,256]{1,0:T(8,128)(2,1)S(1)} %bitcast.11, s32[1,8,128]{2,1,0:T(8,128)S(1)} %scatter.4.list_ref, bf16[576,2048]{1,0:T(8,128)(2,1)} %enc_ref.1), custom_call_target="tpu_custom_call" | custom-call | tf_op jit(solution)/shard_map/pallas_call | solution.py:364
  17.8 0.0 copy-start.1
  17.8 1.4 %copy-done.1 = bf16[16,576,128]{2,1,0:T(8,128)(2,1)} copy-done((bf16[16,576,128]{2,1,0:T(8,128)(2,1)}, bf16[16,576,128]{2,1,0:T(8,128)(2,1)S(1)}, u32[]{:S(2)}) %copy-start.1) | copy-done | bytes 2359320
  19.2 0.1 reshape.250
  19.3 0.1 convert_reduce_fusion.1
  19.4 0.2 select_reduce_fusion.2
  19.7 0.1 reduce_sum.50
  19.8 0.1 stack.7
  19.9 0.1 convert_reduce_fusion
  20.0 0.1 iota_compare_fusion
  20.1 0.3 select_reduce_fusion
  20.4 0.1 copy.14
  20.5 0.1 broadcast_in_dim.36.hits
  20.5 0.0 copy-done.3
  20.6 110.0 %shard_map.94 = (bf16[33,128,128]{2,1,0:T(8,128)(2,1)S(1)}, bf16[576,1024]{1,0:T(8,128)(2,1)S(1)}, bf16[576,2048]{1,0:T(8,128)(2,1)}, bf16[576,256]{1,0:T(8,128)(2,1)S(1)}) custom-call(s32[2,32]{1,0:T(2,128)S(1)} %pad_add_fusion.table, s32[8,16]{1,0:T(8,128)S(1)} %bitcast.12, f32[32,2,128]{2,1,0:T(2,128)S(1)} %broadcast_in_dim.36.hits, ...), custom_call_target="tpu_custom_call" | custom-call | tf_op jit(solution)/shard_map/pallas_call | solution.py:406
  130.6 0.0 copy-start
  130.6 1.7 %copy-done = bf16[576,2048]{1,0:T(8,128)(2,1)S(1)} copy-done((bf16[576,2048]{1,0:T(8,128)(2,1)S(1)}, bf16[576,2048]{1,0:T(8,128)(2,1)}, u32[]{:S(2)}) %copy-start) | copy-done | bytes 2359320
  132.3 6.6 %shard_map.95 = (bf16[576,2048]{1,0:T(8,128)(2,1)}, f32[1,2048]{1,0:T(1,128)}, bf16[576,2048]{1,0:T(8,128)(2,1)}, bf16[576,256]{1,0:T(8,128)(2,1)}) custom-call(s32[8,16]{1,0:T(8,128)S(1)} %bitcast.13, bf16[576,1024]{1,0:T(8,128)(2,1)S(1)} %get-tuple-element.30.stream, bf16[33,128,128]{2,1,0:T(8,128)(2,1)S(1)} %get-tuple-element.31.pg, ...), custom_call_target="tpu_custom_call" | custom-call | tf_op jit(solution)/shard_map/pallas_call | solution.py:447
  (14 shorter events, 0.1 us)
Async XLA Ops:
  0.6 19.9 %copy-start.3 = (f32[2048]{0:T(1024)S(1)}, f32[2048]{0:T(1024)}, u32[]{:S(2)}) copy-start(f32[2048]{0:T(1024)} %param.11) | copy-start | bytes 24580
  2.2 1.0 copy-start.2
  17.8 1.4 %copy-start.1 = (bf16[16,576,128]{2,1,0:T(8,128)(2,1)}, bf16[16,576,128]{2,1,0:T(8,128)(2,1)S(1)}, u32[]{:S(2)}) copy-start(bf16[16,576,128]{2,1,0:T(8,128)(2,1)S(1)} %get-tuple-element.29.enc) | copy-start | bytes 7077892
  130.6 1.7 %copy-start = (bf16[576,2048]{1,0:T(8,128)(2,1)S(1)}, bf16[576,2048]{1,0:T(8,128)(2,1)}, u32[]{:S(2)}) copy-start(bf16[576,2048]{1,0:T(8,128)(2,1)} %get-tuple-element.32.gdec_in) | copy-start | bytes 7077892
